TPU v7x, 512 devices: a whole 4x8x8 slice. The times are simulated.
512 devices in a mesh: row: 64 (over x, z, core), col: 8 (over y).
Axes of the slice: x: 4, y: 8, z: 8, core: 2. Of those that a mesh axis runs over, the one named last changes fastest.
Arguments:
- source: bfloat16 [16384, 64], P('row'), may hold values from -4 to 4
- target: bfloat16 [4096, 64], P('col'), may hold values from -4 to 4
- log_source: float32 [16384], P('row'), may hold values from -1.5 to 1.5
- log_target: float32 [4096], P('col'), may hold values from -1.5 to 1.5
Outputs:
- source_map: float32 [16384, 64], P('row')
- target_map: float32 [4096, 64], P('col')
All inputs are finite; a program needn't handle non-finite values.
Results may differ from a plain program's by a relative error of at most 0.0025.
Values sent between devices are 32-bit elements; how exact they have to be, the bound alone decides.
A program may use at most 128 MiB of HBM per device.

v0:
```python
import jax
import jax.numpy as jnp
from jax import lax
from jax.sharding import PartitionSpec as P

ITERS = 4


entropy_weight = 3.0


def merged(part, axis, combine):
    gathered = jax.tree.map(lambda a: lax.all_gather(a, axis), part)

    def take(source):
        return jax.tree.map(lambda a: lax.dynamic_index_in_dim(a, source, 0, False), gathered)

    return lax.fori_loop(
        1, lax.axis_size(axis), lambda source, state: combine(state, take(source)), take(0)
    )


def cost_tile(source, source_norm, target_tile, tile_norms):
    inner = lax.dot_general(
        source, target_tile, (((1,), (1,)), ((), ())), preferred_element_type=jnp.float32
    )
    return source_norm[:, None] + tile_norms[None, :] - 2.0 * inner


def combine_pair(earlier, later):
    highest = jnp.maximum(earlier[0], later[0])
    return (
        highest,
        earlier[1] * jnp.exp(earlier[0] - highest) + later[1] * jnp.exp(later[0] - highest),
    )


def combine_maps(earlier, later):
    highest = jnp.maximum(earlier[0], later[0])
    first_factor = jnp.exp(earlier[0] - highest)
    second_factor = jnp.exp(later[0] - highest)
    return (
        highest,
        earlier[1] * first_factor + later[1] * second_factor,
        earlier[2] * first_factor[:, None] + later[2] * second_factor[:, None],
    )


def per_device(source, target, log_source, log_target):
    sources_here = source.shape[0]
    targets_here = target.shape[0]
    features = source.shape[1]
    tile_width = min(targets_here, 512)
    tile_count = targets_here // tile_width
    target_tiles = target.reshape(tile_count, tile_width, features)
    source_norm = jnp.sum(jnp.square(source.astype(jnp.float32)), axis=1)
    tile_norms = jnp.sum(jnp.square(target.astype(jnp.float32)), axis=1).reshape(
        tile_count, tile_width
    )

    def row_update(col_scaling):

        def row_visitor(carried, portion):
            target_tile, norms, col_part = portion
            scores = (
                col_part[None, :] - cost_tile(source, source_norm, target_tile, norms)
            ) / entropy_weight
            highest = jnp.maximum(carried[0], jnp.max(scores, axis=1))
            summed = carried[1] * jnp.exp(carried[0] - highest) + jnp.sum(
                jnp.exp(scores - highest[:, None]), axis=1
            )
            return ((highest, summed), None)

        initial = (
            jnp.full((sources_here,), -1e30, jnp.float32),
            jnp.zeros((sources_here,), jnp.float32),
        )
        (highest, summed), unused = lax.scan(
            row_visitor,
            initial,
            (target_tiles, tile_norms, col_scaling.reshape(tile_count, tile_width)),
        )
        highest, summed = merged((highest, summed), "col", combine_pair)
        return entropy_weight * log_source - entropy_weight * (highest + jnp.log(summed))

    def col_update(row_scaling):

        def col_visitor(portion):
            target_tile, norms = portion
            scores = (
                row_scaling[:, None] - cost_tile(source, source_norm, target_tile, norms)
            ) / entropy_weight
            highest = jnp.max(scores, axis=0)
            return (highest, jnp.sum(jnp.exp(scores - highest[None, :]), axis=0))

        highest, summed = lax.map(col_visitor, (target_tiles, tile_norms))
        highest, summed = merged(
            (highest.reshape(targets_here), summed.reshape(targets_here)), "row", combine_pair
        )
        return entropy_weight * log_target - entropy_weight * (highest + jnp.log(summed))

    col_scaling = jnp.zeros((targets_here,), jnp.float32)
    row_scaling = jnp.zeros((sources_here,), jnp.float32)
    for iteration in range(ITERS):
        row_scaling = row_update(col_scaling)
        if iteration + 1 < ITERS:
            col_scaling = col_update(row_scaling)
    col_scaling = col_update(row_scaling)

    def target_visitor(portion):
        target_tile, norms = portion
        scores = (
            row_scaling[:, None] - cost_tile(source, source_norm, target_tile, norms)
        ) / entropy_weight
        highest = jnp.max(scores, axis=0)
        weights = jnp.exp(scores - highest[None, :]).astype(jnp.bfloat16)
        denominator = jnp.sum(weights.astype(jnp.float32), axis=0)
        numerator = lax.dot_general(
            weights, source, (((0,), (0,)), ((), ())), preferred_element_type=jnp.float32
        )
        return (highest, denominator, numerator)

    highest, denominator, numerator = lax.map(target_visitor, (target_tiles, tile_norms))
    highest, denominator, numerator = merged(
        (
            highest.reshape(targets_here),
            denominator.reshape(targets_here),
            numerator.reshape(targets_here, features),
        ),
        "row",
        combine_maps,
    )
    target_map = numerator / denominator[:, None]

    def source_visitor(carried, portion):
        target_tile, norms, col_part = portion
        scores = (
            col_part[None, :] - cost_tile(source, source_norm, target_tile, norms)
        ) / entropy_weight
        highest = jnp.maximum(carried[0], jnp.max(scores, axis=1))
        rescale = jnp.exp(carried[0] - highest)
        weights = jnp.exp(scores - highest[:, None]).astype(jnp.bfloat16)
        denominator = carried[1] * rescale + jnp.sum(weights.astype(jnp.float32), axis=1)
        numerator = carried[2] * rescale[:, None] + jnp.dot(
            weights, target_tile, preferred_element_type=jnp.float32
        )
        return ((highest, denominator, numerator), None)

    initial = (
        jnp.full((sources_here,), -1e30, jnp.float32),
        jnp.zeros((sources_here,), jnp.float32),
        jnp.zeros((sources_here, features), jnp.float32),
    )
    (highest, denominator, numerator), unused = lax.scan(
        source_visitor,
        initial,
        (target_tiles, tile_norms, col_scaling.reshape(tile_count, tile_width)),
    )
    highest, denominator, numerator = merged((highest, denominator, numerator), "col", combine_maps)
    source_map = numerator / denominator[:, None]
    return (source_map, target_map)


def solution(mesh):
    in_specs = (P("row", None), P("col", None), P("row"), P("col"))
    out_specs = (P("row", None), P("col", None))
    return jax.shard_map(
        per_device, mesh=mesh, in_specs=in_specs, out_specs=out_specs, check_vma=False
    )
```

profile of v0, /device:TPU:1, one launch (start us, length us, event | category | flops | bytes accessed | tf_op | source)
XLA Modules:
  0.0 739.1 jit_solution(485640343741031872)
XLA Ops:
  8.9 1.2 fusion.3
  10.3 13.8 %all-gather.17 = f32[8,1,256]{2,1,0:T(1,128)S(1)} all-gather(f32[1,1,256]{2,1,0:T(1,128)S(1)} %bitcast.250), channel_id=1, replica_groups=mesh['row'=64,'col'=8] {'col'}, dimensions={0}, use_global_device_ids=true | all-gather | bytes 9216 | tf_op jit(solution)/shard_map/all_gather | solution.py:13
  24.2 10.5 %all-gather.16 = f32[8,1,256]{2,1,0:T(1,128)S(1)} all-gather(f32[1,1,256]{2,1,0:T(1,128)S(1)} %bitcast.241), channel_id=2, replica_groups=mesh['row'=64,'col'=8] {'col'}, dimensions={0}, use_global_device_ids=true | all-gather | bytes 9216 | tf_op jit(solution)/shard_map/all_gather | solution.py:13
  36.1 63.6 %all-gather.19 = f32[64,1,512]{2,1,0:T(1,128)S(1)} all-gather(f32[1,1,512]{2,1,0:T(1,128)S(1)} %bitcast.247), channel_id=4, replica_groups=mesh['row'=64,'col'=8] {'row'}, dimensions={0}, use_global_device_ids=true | all-gather | bytes 133120 | tf_op jit(solution)/shard_map/all_gather | solution.py:13
  99.7 48.8 %all-gather.18 = f32[64,1,512]{2,1,0:T(1,128)S(1)} all-gather(f32[1,1,512]{2,1,0:T(1,128)S(1)} %bitcast.237), channel_id=3, replica_groups=mesh['row'=64,'col'=8] {'row'}, dimensions={0}, use_global_device_ids=true | all-gather | bytes 133120 | tf_op jit(solution)/shard_map/all_gather | solution.py:13
  148.5 3.7 while.113
  153.2 10.7 %all-gather.20 = f32[8,1,256]{2,1,0:T(1,128)S(1)} all-gather(f32[1,1,256]{2,1,0:T(1,128)S(1)} %bitcast.242), channel_id=5, replica_groups=mesh['row'=64,'col'=8] {'col'}, dimensions={0}, use_global_device_ids=true | all-gather | bytes 9216 | tf_op jit(solution)/shard_map/all_gather | solution.py:13
  164.0 10.4 %all-gather.21 = f32[8,1,256]{2,1,0:T(1,128)S(1)} all-gather(f32[1,1,256]{2,1,0:T(1,128)S(1)} %bitcast.251), channel_id=1, replica_groups=mesh['row'=64,'col'=8] {'col'}, dimensions={0}, use_global_device_ids=true | all-gather | bytes 9216 | tf_op jit(solution)/shard_map/all_gather | solution.py:13
  175.8 54.6 %all-gather.23 = f32[64,1,512]{2,1,0:T(1,128)S(1)} all-gather(f32[1,1,512]{2,1,0:T(1,128)S(1)} %bitcast.248), channel_id=7, replica_groups=mesh['row'=64,'col'=8] {'row'}, dimensions={0}, use_global_device_ids=true | all-gather | bytes 133120 | tf_op jit(solution)/shard_map/all_gather | solution.py:13
  230.5 48.8 %all-gather.22 = f32[64,1,512]{2,1,0:T(1,128)S(1)} all-gather(f32[1,1,512]{2,1,0:T(1,128)S(1)} %bitcast.238), channel_id=6, replica_groups=mesh['row'=64,'col'=8] {'row'}, dimensions={0}, use_global_device_ids=true | all-gather | bytes 133120 | tf_op jit(solution)/shard_map/all_gather | solution.py:13
  279.2 3.7 while.229
  284.0 10.7 %all-gather.24 = f32[8,1,256]{2,1,0:T(1,128)S(1)} all-gather(f32[1,1,256]{2,1,0:T(1,128)S(1)} %bitcast.243), channel_id=8, replica_groups=mesh['row'=64,'col'=8] {'col'}, dimensions={0}, use_global_device_ids=true | all-gather | bytes 9216 | tf_op jit(solution)/shard_map/all_gather | solution.py:13
  294.8 10.4 %all-gather.25 = f32[8,1,256]{2,1,0:T(1,128)S(1)} all-gather(f32[1,1,256]{2,1,0:T(1,128)S(1)} %bitcast.252), channel_id=1, replica_groups=mesh['row'=64,'col'=8] {'col'}, dimensions={0}, use_global_device_ids=true | all-gather | bytes 9216 | tf_op jit(solution)/shard_map/all_gather | solution.py:13
  306.6 54.6 %all-gather.27 = f32[64,1,512]{2,1,0:T(1,128)S(1)} all-gather(f32[1,1,512]{2,1,0:T(1,128)S(1)} %bitcast.249), channel_id=10, replica_groups=mesh['row'=64,'col'=8] {'row'}, dimensions={0}, use_global_device_ids=true | all-gather | bytes 133120 | tf_op jit(solution)/shard_map/all_gather | solution.py:13
  361.2 48.8 %all-gather.26 = f32[64,1,512]{2,1,0:T(1,128)S(1)} all-gather(f32[1,1,512]{2,1,0:T(1,128)S(1)} %bitcast.239), channel_id=9, replica_groups=mesh['row'=64,'col'=8] {'row'}, dimensions={0}, use_global_device_ids=true | all-gather | bytes 133120 | tf_op jit(solution)/shard_map/all_gather | solution.py:13
  410.0 3.7 while.231
  414.8 10.7 %all-gather.28 = f32[8,1,256]{2,1,0:T(1,128)S(1)} all-gather(f32[1,1,256]{2,1,0:T(1,128)S(1)} %bitcast.244), channel_id=11, replica_groups=mesh['row'=64,'col'=8] {'col'}, dimensions={0}, use_global_device_ids=true | all-gather | bytes 9216 | tf_op jit(solution)/shard_map/all_gather | solution.py:13
  425.5 10.4 %all-gather.29 = f32[8,1,256]{2,1,0:T(1,128)S(1)} all-gather(f32[1,1,256]{2,1,0:T(1,128)S(1)} %bitcast.253), channel_id=1, replica_groups=mesh['row'=64,'col'=8] {'col'}, dimensions={0}, use_global_device_ids=true | all-gather | bytes 9216 | tf_op jit(solution)/shard_map/all_gather | solution.py:13
  437.4 1.6 fusion.16
  439.0 54.6 %all-gather.30 = f32[64,1,512]{2,1,0:T(1,128)S(1)} all-gather(f32[1,1,512]{2,1,0:T(1,128)S(1)} %bitcast.236), channel_id=12, replica_groups=mesh['row'=64,'col'=8] {'row'}, dimensions={0}, use_global_device_ids=true | all-gather | bytes 133120 | tf_op jit(solution)/shard_map/all_gather | solution.py:13
  493.6 48.8 %all-gather.34 = f32[64,1,512]{2,1,0:T(1,128)S(1)} all-gather(f32[1,1,512]{2,1,0:T(1,128)S(1)} %bitcast.246), channel_id=16, replica_groups=mesh['row'=64,'col'=8] {'row'}, dimensions={0}, use_global_device_ids=true | all-gather | bytes 133120 | tf_op jit(solution)/shard_map/all_gather | solution.py:13
  542.4 47.2 %all-gather.31 = f32[64,1,512]{2,1,0:T(1,128)S(1)} all-gather(f32[1,1,512]{2,1,0:T(1,128)S(1)} %bitcast.245), channel_id=13, replica_groups=mesh['row'=64,'col'=8] {'row'}, dimensions={0}, use_global_device_ids=true | all-gather | bytes 133120 | tf_op jit(solution)/shard_map/all_gather | solution.py:13
  589.7 3.7 while.233
  594.5 10.7 %all-gather.33 = f32[8,1,256]{2,1,0:T(1,128)S(1)} all-gather(f32[1,1,256]{2,1,0:T(1,128)S(1)} %bitcast.254), channel_id=1, replica_groups=mesh['row'=64,'col'=8] {'col'}, dimensions={0}, use_global_device_ids=true | all-gather | bytes 9216 | tf_op jit(solution)/shard_map/all_gather | solution.py:13
  605.2 10.5 %all-gather.32 = f32[8,1,256]{2,1,0:T(1,128)S(1)} all-gather(f32[1,1,256]{2,1,0:T(1,128)S(1)} %bitcast.240), channel_id=14, replica_groups=mesh['row'=64,'col'=8] {'col'}, dimensions={0}, use_global_device_ids=true | all-gather | bytes 9216 | tf_op jit(solution)/shard_map/all_gather | solution.py:13
  615.8 19.6 %all-gather.13 = f32[2048,64]{0,1:T(8,128)S(1)} all-gather(f32[256,64]{0,1:T(8,128)S(1)} %convolution_add_fusion), channel_id=15, replica_groups=mesh['row'=64,'col'=8] {'col'}, dimensions={0}, use_global_device_ids=true | all-gather | bytes 589824 | tf_op jit(solution)/shard_map/all_gather | solution.py:13
  635.9 1.6 while.234
  639.3 12.2 %copy.19 = f32[32768,64]{1,0:T(8,128)} copy(f32[32768,64]{0,1:T(8,128)} %all-gather.37.cloned.1.call-done) | data formatting | bytes 16777216 | tf_op jit(solution)/shard_map/while | solution.py:18
  651.5 80.0 %while.235 = (s32[]{:T(128)}, f32[512]{0:T(512)S(1)}, f32[512]{0:T(512)S(1)}, f32[512,64]{1,0:T(8,128)S(1)}, f32[64,512]{1,0:T(8,128)S(1)}, /*index=5*/f32[64,51...) while((s32[]{:T(128)}, f32[512]{0:T(512)S(1)}, f32[512]{0:T(512)S(1)}, ...), condition=%wide.region_40.41_spmd, body=%wide.region_39.40_spmd.sunk | while | flops 101381 | bytes 422031 | solution.py:18
  651.5 1.2 fusion.26
  652.8 1.2 fusion.26
  654.1 1.2 fusion.26
  (862 shorter events, 99.8 us)
Async XLA Ops:
  7.2 608.5 %copy-start = (bf16[512,64]{0,1:T(8,128)(2,1)S(1)}, bf16[512,64]{0,1:T(8,128)(2,1)}, u32[]{:S(2)}) copy-start(bf16[512,64]{0,1:T(8,128)(2,1)} %param.25) | copy-start | bytes 196612
  7.2 631.1 %all-gather.37.cloned.1.call-start = ((), (), s32[]{:S(2)}) async-start(), calls=%async_computation | async-start | bytes 8519680 | tf_op jit(solution)/shard_map/all_gather | solution.py:13
Sparse Core Ops, SparseCore 0:
  439.1 90.8 all-gather.36
where the time goes:
time: 754 us; the launch traced here: 739 us
  blocking collectives  598 us (79%)
  other arithmetic  95.8 us (13%)
  local copies, waits for them, and re-layouts  18.1 us (2%)
  between operations  14.3 us (2%)
  loops' own time  9.33 us (1%)
    all_gather x20, blocking collectives, merged(): gathered = jax.tree.map(lambda a: lax.all_gather(a, axis), part)  598 us
    add x70, other arithmetic, combine_maps(): earlier[2] * first_factor[:, None] + later[2] * second_factor[:, None]  77.1 us
  transfers between devices with their start and end apart: 1, of which 0 were waited for; matrix products, arithmetic and copies ran while one was open for 1% of the time, Pallas kernels for 0%

commit v1 on v0

v1 whole, which is shorter than its diff:
```python
import functools

import jax
import jax.numpy as jnp
from jax import lax
from jax.experimental import pallas as pl
from jax.experimental.pallas import tpu as pltpu
from jax.sharding import PartitionSpec as P

ITERS = 4
EPS = 3.0
LOG2E = 1.4426950408889634
SCALE = LOG2E / EPS
SHIFT = 40.0

NX, NZ, NC, NY = 4, 8, 2, 8
NG = NX * NC
S, T, D = 256, 512, 64
BLK = 64
NB = T // BLK
F32, BF16 = jnp.float32, jnp.bfloat16
MESH = pl.DeviceIdType.MESH
RING8 = (4, 3, 5, 2, 6, 1, 7)
PLANE = tuple((dx, dc) for dx in (2, 1, 3) for dc in (1, 0)) + ((0, 1),)

PHASES = ("y1", "y2", "y3", "y4", "yg", "p1", "p2", "p3", "p4", "z1", "den", "num", "map", "src", "fa", "tgt", "fwd")
IDX = {name: i for i, name in enumerate(PHASES)}


def iota(shape, dim):
    return lax.broadcasted_iota(jnp.int32, shape, dim)


def lse2(slots):
    highest = jnp.max(slots, axis=0)
    return highest + jnp.log2(jnp.sum(jnp.exp2(slots - highest[None]), axis=0))


def nt(a, b):
    return lax.dot_general(a, b, (((1,), (1,)), ((), ())), preferred_element_type=F32)


def nn(a, b):
    return lax.dot_general(a, b, (((1,), (0,)), ((), ())), preferred_element_type=F32)


def pack(column, first):
    groups = column.reshape(BLK // 8, 8, 1)
    shape = (BLK // 8, 8, 128)
    return jnp.sum(jnp.where(iota(shape, 2) == iota(shape, 0) + first, groups, 0.0), axis=0)


def unpack(packed, first):
    shape = (BLK // 8, 8, 128)
    picked = jnp.where(iota(shape, 2) == iota(shape, 0) + first, packed[None], 0.0)
    return jnp.sum(picked, axis=2, keepdims=True).reshape(BLK, 1)


def as_column(row):
    parts = []
    for h in range(S // 128):
        part = row[:, h * 128 : (h + 1) * 128]
        diagonal = iota((128, 128), 0) == iota((128, 128), 1)
        parts.append(jnp.sum(jnp.where(diagonal, part, 0.0), axis=1, keepdims=True))
    return jnp.concatenate(parts, axis=0)


def kernel(
    src_ref, tgt_ref, ls_ref, lt_ref, out_s, out_t,
    y1, y2, y3, y4, yg, p1, p2, p3, p4, z1, den, num, mapped, src_all, fa, tgt_all,
    numt, mt_own, k_ref, mf, wb, ste, vcol, ssem, rsem,
):
    row, y = lax.axis_index("row"), lax.axis_index("col")
    x, z, c = row // (NZ * NC), lax.rem(row // NC, NZ), lax.rem(row, NC)
    g = x * NC + c

    def place(px, pz, pc, py):
        return ((px * NZ + pz) * NC + pc, py)

    y_peers = [place(x, z, c, lax.rem(y + d, NY)) for d in RING8]
    z_peers = [place(x, lax.rem(z + d, NZ), c, y) for d in RING8]
    g_pos = [(lax.rem(x + dx, NX), lax.rem(c + dc, NC)) for dx, dc in PLANE]
    g_peers = [place(px, z, pc, y) for px, pc in g_pos]
    g_index = [px * NC + pc for px, pc in g_pos]

    barrier = pltpu.get_barrier_semaphore()
    for peer in y_peers + z_peers + g_peers:
        pl.semaphore_signal(barrier, inc=1, device_id=peer, device_id_type=MESH)

    def send(name, source, target, peer):
        i = IDX[name]
        pltpu.make_async_remote_copy(
            src_ref=source, dst_ref=target, send_sem=ssem.at[i], recv_sem=rsem.at[i],
            device_id=peer, device_id_type=MESH,
        ).start()

    def share(name, buf, me, peers, value=None):
        if value is not None:
            buf[me] = value
        for peer in peers:
            send(name, buf.at[me], buf.at[me], peer)

    def landed(name, buf):
        span = buf.at[pl.ds(0, 7)]
        pltpu.make_async_copy(span, span, rsem.at[IDX[name]]).wait()

    def sent(name, buf):
        span = buf.at[pl.ds(0, 7)]
        pltpu.make_async_copy(span, span, ssem.at[IDX[name]]).wait()

    src, tgt = src_ref[...], tgt_ref[...]
    eye = (iota((D, D), 0) == iota((D, D), 1)).astype(BF16)
    src_t = nt(eye, src)
    src_norm = jnp.sum(src_t * src_t, axis=0, keepdims=True)
    tgt_f = tgt.astype(F32)
    tgt_norm = jnp.sum(tgt_f * tgt_f, axis=1, keepdims=True)
    scores = (src_norm + tgt_norm - 2.0 * nt(tgt, src)) * (-SCALE)
    mt_own[...] = scores
    highest = jnp.max(scores, axis=0, keepdims=True)
    partial = highest + jnp.log2(jnp.sum(jnp.exp2(scores - highest), axis=0, keepdims=True))
    src_all[z] = src_t
    tgt_t = nt(eye, tgt)
    tgt_all[0, y] = tgt_t[: D // 2]
    tgt_all[1, y] = tgt_t[D // 2 :]

    pl.semaphore_wait(barrier, 21)
    share("y1", y1, y, y_peers, partial)
    share("src", src_all, z, z_peers)
    for peer in y_peers:
        send("tgt", tgt_all.at[c, y], tgt_all.at[c, y], peer)

    log_a = ls_ref[...] * LOG2E
    lanes_of = (iota((8, T), 1) % 8 == iota((8, T), 0)).astype(F32)
    spread = (iota((T, 128), 0) // 8 == iota((T, 128), 1)).astype(F32)
    log_b = lax.dot_general(
        lt_ref[...] * LOG2E * lanes_of, spread, (((1,), (0,)), ((), ())),
        preferred_element_type=F32, precision=lax.Precision.HIGHEST,
    )
    mass_b = jnp.exp2(log_b)

    landed("y1", y1)
    f_own = log_a - lse2(y1[...])

    packed = jnp.zeros((8, 128), F32)
    for b in range(NB):
        s = mt_own[b * BLK : (b + 1) * BLK, :] + f_own
        highest = jnp.max(s, axis=1, keepdims=True)
        total = jnp.sum(jnp.exp2(s - highest), axis=1, keepdims=True)
        packed = packed + pack(highest + jnp.log2(total), b * (BLK // 8))
    share("p1", p1, g, g_peers, packed)
    share("fa", fa, z, z_peers, jnp.concatenate([f_own, log_a], axis=1))
    landed("p1", p1)
    share("z1", z1, z, z_peers, lse2(p1[...]))

    landed("fa", fa)
    landed("src", src_all)
    mass_a = jnp.exp2(fa[:, :, S:])
    ste[D:, :] = jnp.ones((D, NZ * S), BF16)

    def fill(zz, carry):
        block = src_all[zz]
        norm = jnp.sum(block * block, axis=0, keepdims=True)
        low = block.astype(BF16)
        inner = nn(tgt_ref[...], low)
        t32 = tgt_ref[...].astype(F32)
        tn = jnp.sum(t32 * t32, axis=1, keepdims=True)
        first = fa[zz][:, :S] + SHIFT
        k_ref[zz] = (norm + tn - 2.0 * inner) * (-SCALE) + first
        ste[pl.ds(0, D), pl.ds(pl.multiple_of(zz * S, S), S)] = low
        return carry

    lax.fori_loop(0, NZ, fill, 0)

    landed("z1", z1)
    g1 = log_b - lse2(z1[...])

    def rows_of(values):
        return jnp.sum(values, axis=1, keepdims=True)

    def build(b, acc):
        span = pl.ds(pl.multiple_of(b * BLK, BLK), BLK)
        block = jnp.exp2(k_ref[:, span, :] + unpack(g1, b * (BLK // 8))[None])
        k_ref[:, span, :] = block
        return acc + jnp.sum(block.reshape(NZ, BLK // 8, 8, S), axis=1)

    def row_pass(v):
        def body(b, acc):
            span = pl.ds(pl.multiple_of(b * BLK, BLK), BLK)
            block = k_ref[:, span, :] * unpack(v, b * (BLK // 8))[None]
            return acc + jnp.sum(block.reshape(NZ, BLK // 8, 8, S), axis=1)

        return lax.fori_loop(0, NB, body, jnp.zeros((NZ, 8, S), F32))

    def col_pass(u, keep=False):
        def body(b, acc):
            span = pl.ds(pl.multiple_of(b * BLK, BLK), BLK)
            block = k_ref[:, span, :] * u
            if keep:
                for zz in range(NZ):
                    wb[span, zz * S : (zz + 1) * S] = block[zz].astype(BF16)
            t = jnp.sum(block, axis=0)
            t = t[:, :128] + t[:, 128:]
            return acc + pack(jnp.sum(t, axis=1, keepdims=True), b * (BLK // 8))

        return lax.fori_loop(0, NB, body, jnp.zeros((8, 128), F32))

    def exchange_rows(name, buf, acc):
        share(name, buf, y, y_peers, rows_of(acc))

    def scaling_u(name, buf):
        landed(name, buf)
        return mass_a / jnp.sum(buf[...], axis=0)

    used = iota((8, 128), 1) < T // 8

    def scaling_v(name, buf):
        landed(name, buf)
        return jnp.where(used, mass_b / jnp.sum(buf[...], axis=0), 1.0)

    exchange_rows("y2", y2, lax.fori_loop(0, NB, build, jnp.zeros((NZ, 8, S), F32)))
    i = IDX["tgt"]
    span = tgt_all.at[0, pl.ds(0, 7)]
    pltpu.make_async_copy(span, span, rsem.at[i]).wait()
    sibling = place(x, z, 1 - c, y)
    for d in RING8:
        other = lax.rem(y + d, NY)
        send("fwd", tgt_all.at[c, other], tgt_all.at[c, other], sibling)
    u = scaling_u("y2", y2)
    share("p2", p2, g, g_peers, col_pass(u))
    i = IDX["fwd"]
    pltpu.make_async_copy(span, span, rsem.at[i]).wait()
    v = scaling_v("p2", p2)

    exchange_rows("y3", y3, row_pass(v))

    def full(yy, carry):
        block = jnp.concatenate([tgt_all[0, yy], tgt_all[1, yy]], axis=0)
        norm = jnp.sum(block * block, axis=0, keepdims=True)
        s32 = src_ref[...].astype(F32)
        sn = jnp.sum(s32 * s32, axis=1, keepdims=True)
        mf[yy] = (sn + norm - 2.0 * nn(src_ref[...], block.astype(BF16))) * (-SCALE)
        return carry

    lax.fori_loop(0, NY, full, 0)
    u = scaling_u("y3", y3)
    share("p3", p3, g, g_peers, col_pass(u))
    v = scaling_v("p3", p3)

    exchange_rows("y4", y4, row_pass(v))
    u = scaling_u("y4", y4)
    share("p4", p4, g, g_peers, col_pass(u, keep=True))
    weighted = nt(ste[...], wb[...])
    den[g] = weighted[D : D + 1]
    for n in range(NG):
        numt[n] = weighted[n * 8 : n * 8 + 8]
    num[g] = numt[g]
    for peer, index in zip(g_peers, g_index):
        send("den", den.at[g], den.at[g], peer)
        send("num", numt.at[index], num.at[g], peer)

    y4_own = jnp.sum(y4[:, z], axis=0)
    f_last = as_column(f_own + log_a - jnp.log2(y4_own) + SHIFT)

    def add_f(yy, carry):
        mf[yy] = mf[yy] + f_last
        return carry

    lax.fori_loop(0, NY, add_f, 0)
    g4 = g1 + jnp.log2(scaling_v("p4", p4))
    over = (iota((128, T), 0) == iota((128, T), 1) // 8).astype(F32)
    g4_rows = lax.dot_general(
        g4, over, (((1,), (0,)), ((), ())), preferred_element_type=F32, precision=lax.Precision.HIGHEST
    )
    g4_row = jnp.sum(g4_rows * lanes_of, axis=0, keepdims=True)
    share("yg", yg, y, y_peers, g4_row)

    landed("den", den)
    landed("num", num)
    share("map", mapped, g, g_peers, jnp.sum(num[...], axis=0) / jnp.sum(den[...], axis=0))

    landed("yg", yg)

    def finish(yy, acc):
        block = jnp.concatenate([tgt_all[0, yy], tgt_all[1, yy], jnp.ones((D, T), F32)], axis=0)
        weight = jnp.exp2(mf[yy] + yg[yy]).astype(BF16)
        return acc + nt(weight, block.astype(BF16))

    both = lax.fori_loop(0, NY, finish, jnp.zeros((S, 2 * D), F32))
    out_s[...] = both[:, :D] / both[:, D:]

    landed("map", mapped)
    for n in range(NG):
        out_t[n * 8 : n * 8 + 8, :] = mapped[n]

    for name, buf in (
        ("y1", y1), ("y2", y2), ("y3", y3), ("y4", y4), ("yg", yg), ("p1", p1), ("p2", p2), ("p3", p3), ("p4", p4),
        ("z1", z1), ("den", den), ("num", num), ("map", mapped), ("src", src_all), ("fa", fa),
        ("tgt", tgt_all.at[0]), ("fwd", tgt_all.at[0]),
    ):
        sent(name, buf)


def per_device(source, target, log_source, log_target):
    vmem = pl.BlockSpec(memory_space=pltpu.VMEM)
    n = len(PHASES)
    scratch = [
        pltpu.VMEM((NY, 1, S), F32),
        pltpu.VMEM((NY, NZ, 1, S), F32),
        pltpu.VMEM((NY, NZ, 1, S), F32),
        pltpu.VMEM((NY, NZ, 1, S), F32),
        pltpu.VMEM((NY, 1, T), F32),
        pltpu.VMEM((NG, 8, 128), F32),
        pltpu.VMEM((NG, 8, 128), F32),
        pltpu.VMEM((NG, 8, 128), F32),
        pltpu.VMEM((NG, 8, 128), F32),
        pltpu.VMEM((NZ, 8, 128), F32),
        pltpu.VMEM((NG, 1, T), F32),
        pltpu.VMEM((NG, 8, T), F32),
        pltpu.VMEM((NG, 8, T), F32),
        pltpu.VMEM((NZ, D, S), F32),
        pltpu.VMEM((NZ, 1, 2 * S), F32),
        pltpu.VMEM((2, NY, D // 2, T), F32),
        pltpu.VMEM((NG, 8, T), F32),
        pltpu.VMEM((T, S), F32),
        pltpu.VMEM((NZ, T, S), F32),
        pltpu.VMEM((NY, S, T), F32),
        pltpu.VMEM((T, NZ * S), BF16),
        pltpu.VMEM((2 * D, NZ * S), BF16),
        pltpu.VMEM((8, 128), F32),
        pltpu.SemaphoreType.DMA((n,)),
        pltpu.SemaphoreType.DMA((n,)),
    ]
    source_map, target_map = pl.pallas_call(
        kernel,
        out_shape=(jax.ShapeDtypeStruct((S, D), F32), jax.ShapeDtypeStruct((D, T), F32)),
        in_specs=[vmem] * 4,
        out_specs=(vmem, vmem),
        scratch_shapes=scratch,
        compiler_params=pltpu.CompilerParams(
            collective_id=0, has_side_effects=True, vmem_limit_bytes=48 * 1024 * 1024
        ),
    )(source, target, log_source.reshape(1, S), log_target.reshape(1, T))
    return source_map, target_map.T


def solution(mesh):
    in_specs = (P("row", None), P("col", None), P("row"), P("col"))
    out_specs = (P("row", None), P("col", None))
    return jax.shard_map(
        per_device, mesh=mesh, in_specs=in_specs, out_specs=out_specs, check_vma=False
    )
```

time: 754 us -> 72.7 us (0.10); the launches traced: 739 us -> 72.5 us
  blocking collectives: 598 us -> 0 us
  other arithmetic: 95.8 us -> 0 us
  Pallas kernels: 0 us -> 68.9 us
  local copies, waits for them, and re-layouts: 18.1 us -> 2.95 us
  between operations: 14.3 us -> 0.68 us
  loops' own time: 9.33 us -> 0 us
    all_gather x20 -> x0, blocking collectives: 598 us -> none  [merged(): gathered = jax.tree.map(lambda a: lax.all_gather(a, axis), part)]
    add x424 -> x0, other arithmetic: 84.3 us -> none  [the longest x70 77.1 us: combine_maps(): earlier[2] * first_factor[:, None] + later[2] * second_factor[:, None]]
    pallas_call x0 -> x1, Pallas kernels: none -> 68.9 us  [per_device(): pl.pallas_call(kernel, out_shape=(jax.ShapeDtypeStruct((S, D), F32), jax....]
    while x6 -> x0, local copies, waits for them, and re-layouts: 13 us -> none  [merged(): lax.fori_loop(1, lax.axis_size(axis), lambda source, state: combine(state...]
    another operation x10 -> x0, loops' own time: 9.33 us -> none  [merged(): lax.fori_loop(1, lax.axis_size(axis), lambda source, state: combine(state...]
  transfers between devices with their start and end apart: 1 -> 0, of which waited for: 0 -> 0; matrix products, arithmetic and copies ran while one was open for 1% -> 0% of each run, Pallas kernels for 0% -> 0%
where the time goes in v1:
time: 72.7 us; the launch traced here: 72.5 us
  Pallas kernels  68.9 us (95%)
  local copies, waits for them, and re-layouts  2.95 us (4%)
    pallas_call x1, Pallas kernels, per_device(): pl.pallas_call(kernel, out_shape=(jax.ShapeDtypeStruct((S, D), F32), jax....  68.9 us
    unnamed x10, local copies, waits for them, and re-layouts  2.95 us

profile of v1, /device:TPU:1, one launch (start us, length us, event | category | flops | bytes accessed | tf_op | source)
XLA Modules:
  0.0 72.5 jit_solution(8603634396795850984)
XLA Ops:
  0.6 0.0 copy-start.2
  0.6 0.9 %copy.6.src_ref = bf16[256,64]{1,0:T(8,128)(2,1)S(1)} copy(bf16[256,64]{0,1:T(8,128)(2,1)} %param.4) | data formatting | bytes 65536 | tf_op args[0]
  1.5 0.0 copy-done.2
  1.6 0.0 copy-start
  1.6 0.0 copy-start.1
  1.6 0.1 copy.7.tgt_ref
  1.7 0.5 copy-done
  2.2 0.0 copy-done.1
  2.3 68.9 %shard_map.59 = (f32[256,64]{1,0:T(8,128)S(1)}, f32[64,512]{1,0:T(8,128)S(1)}) custom-call(bf16[256,64]{1,0:T(8,128)(2,1)S(1)} %copy.6.src_ref, bf16[512,64]{1,0:T(8,128)(2,1)S(1)} %copy.7.tgt_ref, f32[1,256]{1,0:T(1,128)S(1)} %bitcast.5, f32[1,512]{1,0:T(1,128)S(1)} %bitcast.4), custom_call_target="tpu_custom_call" | custom-call | tf_op jit(solution)/shard_map/pallas_call | solution.py:333
  71.1 0.7 copy.8
  71.8 0.7 copy.10
Async XLA Ops:
  0.6 0.9 %copy-start.2 = (bf16[512,64]{0,1:T(8,128)(2,1)S(1)}, bf16[512,64]{0,1:T(8,128)(2,1)}, u32[]{:S(2)}) copy-start(bf16[512,64]{0,1:T(8,128)(2,1)} %param.5) | copy-start | bytes 196612
  1.6 0.7 copy-start
  1.6 0.7 copy-start.1

commit v2 on v1

v2 whole, which is shorter than its diff:
```python
import jax
import jax.numpy as jnp
from jax import lax
from jax.experimental import pallas as pl
from jax.experimental.pallas import tpu as pltpu
from jax.sharding import PartitionSpec as P

EPS = 3.0
LOG2E = 1.4426950408889634
SCALE = LOG2E / EPS
SHIFT = 40.0

NX, NZ, NC, NY = 4, 8, 2, 8
NG = NX * NC
ZH, YH = 4, 2
NR = NG * 2
FR = 64 // NR
S, T, D = 256, 512, 64
NK = T // 8
F32, BF16 = jnp.float32, jnp.bfloat16
MESH = pl.DeviceIdType.MESH
RING8 = (4, 3, 5, 2, 6, 1, 7)
PLANE = tuple((dx, dc) for dx in (2, 1, 3) for dc in (1, 0)) + ((0, 1),)

PHASES = (
    "y1", "y2", "y3", "y4", "yg", "p1", "z1", "p2", "p3", "p4", "den", "num", "map", "src", "fa", "ga", "tgt", "fwd",
)
IDX = {name: i for i, name in enumerate(PHASES)}


def iota(shape, dim):
    return lax.broadcasted_iota(jnp.int32, shape, dim)


def lse2(slots):
    highest = jnp.max(slots, axis=0)
    return highest + jnp.log2(jnp.sum(jnp.exp2(slots - highest[None]), axis=0))


def nt(a, b):
    return lax.dot_general(a, b, (((1,), (1,)), ((), ())), preferred_element_type=F32)


def nn(a, b):
    return lax.dot_general(a, b, (((1,), (0,)), ((), ())), preferred_element_type=F32)


def tn(a, b):
    return lax.dot_general(a, b, (((0,), (0,)), ((), ())), preferred_element_type=F32)


def norm_rows(points):
    norm = jnp.sum(points * points, axis=0, keepdims=True)
    first = norm.astype(BF16).astype(F32)
    second = (norm - first).astype(BF16).astype(F32)
    third = norm - first - second
    shape = (8, points.shape[1])
    row = iota(shape, 0)
    return jnp.where(row == 0, first, jnp.where(row == 1, second, jnp.where(row == 2, third, 0.0)))


def with_norms_s(points):
    ones = jnp.ones((8, points.shape[1]), F32)
    return jnp.concatenate([points, ones, norm_rows(points)], axis=0).astype(BF16)


def with_norms_t(points):
    ones = jnp.ones((8, points.shape[1]), F32)
    return jnp.concatenate([points * -2.0, norm_rows(points), ones], axis=0).astype(BF16)


def kernel(
    src_ref, tgt_ref, ls_ref, lt_ref, out_s, out_t,
    y1, y2, y3, y4, yg, p1, z1, p2, p3, p4, den, num, mapped, src_all, fa, ga, tgt_all,
    numt, mt_own, k_ref, mf, wb, ste, ssem, rsem,
):
    row, y = lax.axis_index("row"), lax.axis_index("col")
    x, z, c = row // (NZ * NC), lax.rem(row // NC, NZ), lax.rem(row, NC)
    g = x * NC + c
    zp, zi = lax.rem(z, 2), z // 2
    m = g * 2 + zp
    yc, h = lax.rem(y, 4), y // 4

    def place(px, pz, pc, py):
        return ((px * NZ + pz) * NC + pc, py)

    y_peers = [place(x, z, c, lax.rem(y + d, NY)) for d in RING8]
    y4_peers = [place(x, z, c, lax.rem(y + d, NY)) for d in (2, 1, 7)]
    z_peers = [place(x, lax.rem(z + d, NZ), c, y) for d in RING8]
    z4_peers = [place(x, lax.rem(z + d, NZ), c, y) for d in (4, 2, 6)]
    g_pos = [(lax.rem(x + dx, NX), lax.rem(c + dc, NC)) for dx, dc in PLANE]
    g_peers = [place(px, z, pc, y) for px, pc in g_pos]
    z_pair = z + 1 - 2 * zp
    far_pos = [(lax.rem(x + dx, NX), lax.rem(c + dc, NC)) for dx in (2, 1, 3, 0) for dc in (1, 0)]
    r_peers, r_index = [], []
    for dx in (2, 1, 3, 0):
        for pair in (True, False):
            for dc in (1, 0):
                if dx == 0 and dc == 0 and not pair:
                    continue
                px, pc = lax.rem(x + dx, NX), lax.rem(c + dc, NC)
                r_peers.append(place(px, z_pair if pair else z, pc, y))
                r_index.append((px * NC + pc) * 2 + ((1 - zp) if pair else zp))

    barrier = pltpu.get_barrier_semaphore()
    greeted = y_peers + z_peers + g_peers + [place(px, z_pair, pc, y) for px, pc in far_pos[:-1]]
    for peer in greeted:
        pl.semaphore_signal(barrier, inc=1, device_id=peer, device_id_type=MESH)

    def send(name, source, target, peer):
        i = IDX[name]
        pltpu.make_async_remote_copy(
            src_ref=source, dst_ref=target, send_sem=ssem.at[i], recv_sem=rsem.at[i],
            device_id=peer, device_id_type=MESH,
        ).start()

    def share(name, buf, me, peers, value):
        buf[me] = value
        for peer in peers:
            send(name, buf.at[me], buf.at[me], peer)

    def settle(sems, name, buf, n):
        span = buf.at[pl.ds(0, n)]
        pltpu.make_async_copy(span, span, sems.at[IDX[name]]).wait()

    src_t, tgt_t = src_ref[...].astype(F32), tgt_ref[...].astype(F32)
    src_own, tgt_own = with_norms_s(src_t), with_norms_t(tgt_t)
    scores = tn(tgt_own, src_own) * (-SCALE)
    highest = jnp.max(scores, axis=0, keepdims=True)
    partial = highest + jnp.log2(jnp.sum(jnp.exp2(scores - highest), axis=0, keepdims=True))

    pl.semaphore_wait(barrier, len(greeted))
    share("y1", y1, y, y_peers, partial)
    share("src", src_all, zi, z4_peers, src_t)
    tgt_all[0, y] = tgt_t[: D // 2]
    tgt_all[1, y] = tgt_t[D // 2 :]
    for peer in y_peers:
        send("tgt", tgt_all.at[c, y], tgt_all.at[c, y], peer)
    mt_own[...] = scores

    log_a = ls_ref[...] * LOG2E
    lanes_of = (iota((8, T), 1) % 8 == iota((8, T), 0)).astype(F32)
    spread = (iota((T, 128), 0) // 8 == iota((T, 128), 1)).astype(F32)
    log_b_own = lax.dot_general(
        lt_ref[...] * LOG2E * lanes_of, spread, (((1,), (0,)), ((), ())),
        preferred_element_type=F32, precision=lax.Precision.HIGHEST,
    )
    lane = iota((8, 128), 1)

    settle(rsem, "y1", y1, 7)
    f_own = log_a - lse2(y1[...])

    packed = jnp.zeros((8, 128), F32)
    for k in range(NK):
        s = mt_own[8 * k : 8 * k + 8, :] + f_own
        highest = jnp.max(s, axis=1, keepdims=True)
        total = jnp.sum(jnp.exp2(s - highest), axis=1, keepdims=True)
        packed = jnp.where(lane == k, highest + jnp.log2(total), packed)
    share("p1", p1, g, g_peers, packed)
    share("fa", fa, zi, z4_peers, jnp.concatenate([f_own, log_a], axis=1))
    settle(rsem, "p1", p1, 7)
    share("z1", z1, z, z_peers, lse2(p1[...]))

    settle(rsem, "src", src_all, 3)
    settle(rsem, "fa", fa, 3)
    mass_a = jnp.exp2(fa[:, :, S:])
    ste[D:, :] = jnp.ones((D, ZH * S), BF16)
    for zz in range(ZH):
        ste[:D, zz * S : (zz + 1) * S] = src_all[zz].astype(BF16)

    def fill(half, points):
        for zz in range(ZH):
            inner = tn(points, with_norms_s(src_all[zz]))
            k_ref[half, zz] = inner * (-SCALE) + (fa[zz][:, :S] + SHIFT)

    fill(h, tgt_own)
    settle(rsem, "tgt", tgt_all.at[0], 7)
    sibling = place(x, z, 1 - c, y)
    for d in RING8:
        other = lax.rem(y + d, NY)
        send("fwd", tgt_all.at[c, other], tgt_all.at[c, other], sibling)

    def build(half, potential, acc):
        for k in range(NK):
            block = jnp.exp2(k_ref[half, :, 8 * k : 8 * k + 8, :] + potential[:, k : k + 1])
            k_ref[half, :, 8 * k : 8 * k + 8, :] = block
            if acc is not None:
                acc = acc + block
        return acc

    def row_pass(v):
        acc = jnp.zeros((ZH, 8, S), F32)
        for half in range(YH):
            for k in range(NK):
                n = half * NK + k
                acc = acc + k_ref[half, :, 8 * k : 8 * k + 8, :] * v[:, n : n + 1]
        return jnp.sum(acc, axis=1, keepdims=True)

    def col_pass(u, keep=False):
        out = jnp.zeros((8, 128), F32)
        ub = jnp.broadcast_to(u, (ZH, 8, S))
        for half in range(YH):
            for k in range(NK):
                block = k_ref[half, :, 8 * k : 8 * k + 8, :] * ub
                if keep and k % 2 == 0:
                    before = block
                elif keep:
                    for zz in range(ZH):
                        pair = jnp.concatenate([before[zz], block[zz]], axis=0)
                        wb[half, 8 * k - 8 : 8 * k + 8, zz * S : (zz + 1) * S] = pair.astype(BF16)
                t = jnp.sum(block, axis=0)
                t = t[:, :128] + t[:, 128:]
                out = jnp.where(lane == half * NK + k, jnp.sum(t, axis=1, keepdims=True), out)
        return out

    settle(rsem, "z1", z1, 7)
    g1_own = log_b_own - lse2(z1[...])
    acc = build(h, g1_own, jnp.zeros((ZH, 8, S), F32))
    share("y2", y2, y, y_peers, jnp.sum(acc, axis=1, keepdims=True))
    ga[0] = jnp.concatenate([g1_own, log_b_own], axis=0)
    send("ga", ga.at[0], ga.at[1], place(x, z, c, lax.rem(y + 4, NY)))
    settle(rsem, "fwd", tgt_all.at[0], 7)

    def full(yy, carry):
        block = jnp.concatenate([tgt_all[0, yy], tgt_all[1, yy]], axis=0)
        mf[yy] = tn(with_norms_t(block), src_own) * (-SCALE)
        return carry

    other = lax.rem(y + 4, NY)
    fill(1 - h, with_norms_t(jnp.concatenate([tgt_all[0, other], tgt_all[1, other]], axis=0)))
    settle(rsem, "ga", ga, 1)
    g1_far, log_b_far = ga[1][:8], ga[1][8:]

    def both_halves(own, far):
        own, far = own[:, :NK], far[:, :NK]
        return jnp.where(h == 0, jnp.concatenate([own, far], axis=1), jnp.concatenate([far, own], axis=1))

    g1 = both_halves(g1_own, g1_far)
    mass_b = jnp.exp2(both_halves(log_b_own, log_b_far))
    build(1 - h, g1_far, None)

    settle(rsem, "y2", y2, 7)
    u = mass_a / jnp.sum(y2[...], axis=0)
    share("p2", p2, m, r_peers, col_pass(u))
    lax.fori_loop(0, NY, full, 0)
    settle(rsem, "p2", p2, NR - 1)
    v = mass_b / jnp.sum(p2[...], axis=0)

    share("y3", y3, yc, y4_peers, row_pass(v))
    settle(rsem, "y3", y3, 3)
    u = mass_a / jnp.sum(y3[...], axis=0)
    share("p3", p3, m, r_peers, col_pass(u))
    settle(rsem, "p3", p3, NR - 1)
    v = mass_b / jnp.sum(p3[...], axis=0)

    share("y4", y4, yc, y4_peers, row_pass(v))
    settle(rsem, "y4", y4, 3)
    sums = jnp.sum(y4[...], axis=0)
    u = mass_a / sums
    share("p4", p4, m, r_peers, col_pass(u, keep=True))
    weighted = nt(ste[...], wb[h])
    den[m] = weighted[D : D + 1]
    for n in range(NR):
        numt[n] = weighted[n * FR : n * FR + FR]
    num[m] = numt[m]
    for peer, index in zip(r_peers, r_index):
        send("den", den.at[m], den.at[m], peer)
        send("num", numt.at[index], num.at[m], peer)

    f_last = f_own + log_a - jnp.log2(jnp.sum(y4[:, zi], axis=0)) + SHIFT

    def add_f(yy, carry):
        mf[yy] = mf[yy] + f_last
        return carry

    lax.fori_loop(0, NY, add_f, 0)
    settle(rsem, "p4", p4, NR - 1)
    g4 = g1 + jnp.log2(mass_b / jnp.sum(p4[...], axis=0))
    share("yg", yg, yc, y4_peers, g4)

    settle(rsem, "den", den, NR - 1)
    settle(rsem, "num", num, NR - 1)
    share("map", mapped, m, r_peers, jnp.sum(num[...], axis=0) / jnp.sum(den[...], axis=0))

    settle(rsem, "yg", yg, 3)

    def finish(cls, acc):
        potential = yg[cls]
        for half in range(YH):
            yy = cls + 4 * half
            parts = []
            for k in range(NK):
                n = half * NK + k
                parts.append(jnp.exp2(mf[yy, 8 * k : 8 * k + 8, :] + potential[:, n : n + 1]))
            weight = jnp.concatenate(parts, axis=0).astype(BF16)
            block = jnp.concatenate([tgt_all[0, yy], tgt_all[1, yy], jnp.ones((D, T), F32)], axis=0)
            acc = acc + nn(block.astype(BF16), weight)
        return acc

    both = lax.fori_loop(0, 4, finish, jnp.zeros((2 * D, S), F32))
    out_s[...] = both[:D] / both[D:]

    settle(rsem, "map", mapped, NR - 1)
    for n in range(NR):
        out_t[n * FR : n * FR + FR, :] = mapped[n]

    for name, buf, n in (
        ("y1", y1, 7), ("y2", y2, 7), ("y3", y3, 3), ("y4", y4, 3), ("yg", yg, 3), ("p1", p1, 7), ("z1", z1, 7),
        ("p2", p2, NR - 1), ("p3", p3, NR - 1), ("p4", p4, NR - 1), ("den", den, NR - 1), ("num", num, NR - 1),
        ("map", mapped, NR - 1), ("src", src_all, 3), ("fa", fa, 3), ("ga", ga, 1),
        ("tgt", tgt_all.at[0], 7), ("fwd", tgt_all.at[0], 7),
    ):
        settle(ssem, name, buf, n)


def per_device(source, target, log_source, log_target):
    vmem = pl.BlockSpec(memory_space=pltpu.VMEM)
    n = len(PHASES)
    scratch = [
        pltpu.VMEM((NY, 1, S), F32),
        pltpu.VMEM((NY, ZH, 1, S), F32),
        pltpu.VMEM((4, ZH, 1, S), F32),
        pltpu.VMEM((4, ZH, 1, S), F32),
        pltpu.VMEM((4, 8, 128), F32),
        pltpu.VMEM((NG, 8, 128), F32),
        pltpu.VMEM((NZ, 8, 128), F32),
        pltpu.VMEM((NR, 8, 128), F32),
        pltpu.VMEM((NR, 8, 128), F32),
        pltpu.VMEM((NR, 8, 128), F32),
        pltpu.VMEM((NR, 1, T), F32),
        pltpu.VMEM((NR, FR, T), F32),
        pltpu.VMEM((NR, FR, T), F32),
        pltpu.VMEM((ZH, D, S), F32),
        pltpu.VMEM((ZH, 1, 2 * S), F32),
        pltpu.VMEM((2, 16, 128), F32),
        pltpu.VMEM((2, NY, D // 2, T), F32),
        pltpu.VMEM((NR, FR, T), F32),
        pltpu.VMEM((T, S), F32),
        pltpu.VMEM((YH, ZH, T, S), F32),
        pltpu.VMEM((NY, T, S), F32),
        pltpu.VMEM((YH, T, ZH * S), BF16),
        pltpu.VMEM((2 * D, ZH * S), BF16),
        pltpu.SemaphoreType.DMA((n,)),
        pltpu.SemaphoreType.DMA((n,)),
    ]
    source_map, target_map = pl.pallas_call(
        kernel,
        out_shape=(jax.ShapeDtypeStruct((D, S), F32), jax.ShapeDtypeStruct((D, T), F32)),
        in_specs=[vmem] * 4,
        out_specs=(vmem, vmem),
        scratch_shapes=scratch,
        compiler_params=pltpu.CompilerParams(
            collective_id=0, has_side_effects=True, vmem_limit_bytes=48 * 1024 * 1024
        ),
    )(source.T, target.T, log_source.reshape(1, S), log_target.reshape(1, T))
    return source_map.T, target_map.T


def solution(mesh):
    in_specs = (P("row", None), P("col", None), P("row"), P("col"))
    out_specs = (P("row", None), P("col", None))
    return jax.shard_map(
        per_device, mesh=mesh, in_specs=in_specs, out_specs=out_specs, check_vma=False
    )
```

time: 72.7 us -> 67 us (0.922)
  Pallas kernels: 68.9 us -> 62.5 us
    pallas_call x1, Pallas kernels: 68.9 us -> 62.5 us  [per_device(): pl.pallas_call(kernel, out_shape=(jax.ShapeDtypeStruct((D, S), F32), jax....]
where the time goes in v2:
time: 67 us; the launch traced here: 66.7 us
  Pallas kernels  62.5 us (93%)
  local copies, waits for them, and re-layouts  3.56 us (5%)
    pallas_call x1, Pallas kernels, per_device(): pl.pallas_call(kernel, out_shape=(jax.ShapeDtypeStruct((D, S), F32), jax....  62.5 us
    unnamed x10, local copies, waits for them, and re-layouts  3.56 us

profile of v2, /device:TPU:1, one launch (start us, length us, event | category | flops | bytes accessed | tf_op | source)
XLA Modules:
  0.0 66.7 jit_solution(923906831996472649)
XLA Ops:
  0.6 0.0 copy-start.2
  0.6 0.0 copy-start.3
  0.7 0.7 copy-done.2
  1.3 0.0 copy-done.3
  1.3 0.0 copy-start
  1.3 0.8 %copy-done = bf16[512,64]{0,1:T(8,128)(2,1)S(1)} copy-done((bf16[512,64]{0,1:T(8,128)(2,1)S(1)}, bf16[512,64]{0,1:T(8,128)(2,1)}, u32[]{:S(2)}) %copy-start) | copy-done | bytes 65560
  2.2 0.0 copy-start.1
  2.2 0.8 %copy-done.1 = bf16[256,64]{0,1:T(8,128)(2,1)S(1)} copy-done((bf16[256,64]{0,1:T(8,128)(2,1)S(1)}, bf16[256,64]{0,1:T(8,128)(2,1)}, u32[]{:S(2)}) %copy-start.1) | copy-done | bytes 32792
  2.9 62.5 %shard_map.59 = (f32[64,256]{1,0:T(8,128)S(1)}, f32[64,512]{1,0:T(8,128)S(1)}) custom-call(bf16[64,256]{1,0:T(8,128)(2,1)S(1)} %bitcast.9, bf16[64,512]{1,0:T(8,128)(2,1)S(1)} %bitcast.7, f32[1,256]{1,0:T(1,128)S(1)} %bitcast.11, f32[1,512]{1,0:T(1,128)S(1)} %bitcast.10), custom_call_target="tpu_custom_call" | custom-call | tf_op jit(solution)/shard_map/pallas_call | solution.py:346
  65.5 0.6 copy.8
  66.1 0.7 copy.9
Async XLA Ops:
  0.6 0.7 %copy-start.2 = (f32[512]{0:T(512)S(1)}, f32[512]{0:T(512)}, u32[]{:S(2)}) copy-start(f32[512]{0:T(512)} %param.7) | copy-start | bytes 6148
  0.6 0.7 %copy-start.3 = (f32[256]{0:T(256)S(1)}, f32[256]{0:T(256)}, u32[]{:S(2)}) copy-start(f32[256]{0:T(256)} %param.6) | copy-start | bytes 3076
  1.3 0.8 %copy-start = (bf16[512,64]{0,1:T(8,128)(2,1)S(1)}, bf16[512,64]{0,1:T(8,128)(2,1)}, u32[]{:S(2)}) copy-start(bf16[512,64]{0,1:T(8,128)(2,1)} %param.5) | copy-start | bytes 196612
  2.2 0.8 %copy-start.1 = (bf16[256,64]{0,1:T(8,128)(2,1)S(1)}, bf16[256,64]{0,1:T(8,128)(2,1)}, u32[]{:S(2)}) copy-start(bf16[256,64]{0,1:T(8,128)(2,1)} %param.4) | copy-start | bytes 98308

commit v3 on v2

--- a/solution.py
+++ b/solution.py
@@ -24,6 +24,7 @@
 
 PHASES = (
     "y1", "y2", "y3", "y4", "yg", "p1", "z1", "p2", "p3", "p4", "den", "num", "map", "src", "fa", "ga", "tgt", "fwd",
+    "tgb", "fwb",
 )
 IDX = {name: i for i, name in enumerate(PHASES)}
 
@@ -70,9 +71,9 @@
 
 
 def kernel(
-    src_ref, tgt_ref, ls_ref, lt_ref, out_s, out_t,
+    src_hbm, tgt_hbm, ls_hbm, lt_hbm, out_s, out_t,
     y1, y2, y3, y4, yg, p1, z1, p2, p3, p4, den, num, mapped, src_all, fa, ga, tgt_all,
-    numt, mt_own, k_ref, mf, wb, ste, ssem, rsem,
+    numt, mt_own, k_ref, mf, wb, ste, src_ref, tgt_ref, ls_ref, lt_ref, ssem, rsem, isem,
 ):
     row, y = lax.axis_index("row"), lax.axis_index("col")
     x, z, c = row // (NZ * NC), lax.rem(row // NC, NZ), lax.rem(row, NC)
@@ -102,6 +103,14 @@
                 r_peers.append(place(px, z_pair if pair else z, pc, y))
                 r_index.append((px * NC + pc) * 2 + ((1 - zp) if pair else zp))
 
+    loads = [
+        pltpu.make_async_copy(a, b, isem.at[i])
+        for i, (a, b) in enumerate(
+            ((src_hbm, src_ref), (tgt_hbm, tgt_ref), (ls_hbm, ls_ref), (lt_hbm, lt_ref))
+        )
+    ]
+    for load in loads:
+        load.start()
     barrier = pltpu.get_barrier_semaphore()
     greeted = y_peers + z_peers + g_peers + [place(px, z_pair, pc, y) for px, pc in far_pos[:-1]]
     for peer in greeted:
@@ -123,6 +132,8 @@
         span = buf.at[pl.ds(0, n)]
         pltpu.make_async_copy(span, span, sems.at[IDX[name]]).wait()
 
+    for load in loads:
+        load.wait()
     src_t, tgt_t = src_ref[...].astype(F32), tgt_ref[...].astype(F32)
     src_own, tgt_own = with_norms_s(src_t), with_norms_t(tgt_t)
     scores = tn(tgt_own, src_own) * (-SCALE)
@@ -134,8 +145,6 @@
     share("src", src_all, zi, z4_peers, src_t)
     tgt_all[0, y] = tgt_t[: D // 2]
     tgt_all[1, y] = tgt_t[D // 2 :]
-    for peer in y_peers:
-        send("tgt", tgt_all.at[c, y], tgt_all.at[c, y], peer)
     mt_own[...] = scores
 
     log_a = ls_ref[...] * LOG2E
@@ -148,6 +157,8 @@
     lane = iota((8, 128), 1)
 
     settle(rsem, "y1", y1, 7)
+    for peer in y_peers[:3]:
+        send("tgt", tgt_all.at[c, y], tgt_all.at[c, y], peer)
     f_own = log_a - lse2(y1[...])
 
     packed = jnp.zeros((8, 128), F32)
@@ -174,11 +185,15 @@
             k_ref[half, zz] = inner * (-SCALE) + (fa[zz][:, :S] + SHIFT)
 
     fill(h, tgt_own)
-    settle(rsem, "tgt", tgt_all.at[0], 7)
     sibling = place(x, z, 1 - c, y)
-    for d in RING8:
-        other = lax.rem(y + d, NY)
-        send("fwd", tgt_all.at[c, other], tgt_all.at[c, other], sibling)
+
+    def forward(arrived, name, distances):
+        settle(rsem, arrived, tgt_all.at[0], len(distances))
+        for d in distances:
+            other = lax.rem(y + d, NY)
+            send(name, tgt_all.at[c, other], tgt_all.at[c, other], sibling)
+
+    forward("tgt", "fwd", RING8[:3])
 
     def build(half, potential, acc):
         for k in range(NK):
@@ -196,22 +211,23 @@
                 acc = acc + k_ref[half, :, 8 * k : 8 * k + 8, :] * v[:, n : n + 1]
         return jnp.sum(acc, axis=1, keepdims=True)
 
-    def col_pass(u, keep=False):
-        out = jnp.zeros((8, 128), F32)
+    def col_half(half, u, first, out, keep=False):
         ub = jnp.broadcast_to(u, (ZH, 8, S))
-        for half in range(YH):
-            for k in range(NK):
-                block = k_ref[half, :, 8 * k : 8 * k + 8, :] * ub
-                if keep and k % 2 == 0:
-                    before = block
-                elif keep:
-                    for zz in range(ZH):
-                        pair = jnp.concatenate([before[zz], block[zz]], axis=0)
-                        wb[half, 8 * k - 8 : 8 * k + 8, zz * S : (zz + 1) * S] = pair.astype(BF16)
-                t = jnp.sum(block, axis=0)
-                t = t[:, :128] + t[:, 128:]
-                out = jnp.where(lane == half * NK + k, jnp.sum(t, axis=1, keepdims=True), out)
+        for k in range(NK):
+            block = k_ref[half, :, 8 * k : 8 * k + 8, :] * ub
+            if keep and k % 2 == 0:
+                before = block
+            elif keep:
+                for zz in range(ZH):
+                    pair = jnp.concatenate([before[zz], block[zz]], axis=0)
+                    wb[8 * k - 8 : 8 * k + 8, zz * S : (zz + 1) * S] = pair.astype(BF16)
+            t = jnp.sum(block, axis=0)
+            t = t[:, :128] + t[:, 128:]
+            out = jnp.where(lane == first + k, jnp.sum(t, axis=1, keepdims=True), out)
         return out
+
+    def col_pass(u):
+        return col_half(1, u, NK, col_half(0, u, 0, jnp.zeros((8, 128), F32)))
 
     settle(rsem, "z1", z1, 7)
     g1_own = log_b_own - lse2(z1[...])
@@ -219,7 +235,7 @@
     share("y2", y2, y, y_peers, jnp.sum(acc, axis=1, keepdims=True))
     ga[0] = jnp.concatenate([g1_own, log_b_own], axis=0)
     send("ga", ga.at[0], ga.at[1], place(x, z, c, lax.rem(y + 4, NY)))
-    settle(rsem, "fwd", tgt_all.at[0], 7)
+    settle(rsem, "fwd", tgt_all.at[0], 3)
 
     def full(yy, carry):
         block = jnp.concatenate([tgt_all[0, yy], tgt_all[1, yy]], axis=0)
@@ -240,9 +256,10 @@
     build(1 - h, g1_far, None)
 
     settle(rsem, "y2", y2, 7)
+    for peer in y_peers[3:]:
+        send("tgb", tgt_all.at[c, y], tgt_all.at[c, y], peer)
     u = mass_a / jnp.sum(y2[...], axis=0)
     share("p2", p2, m, r_peers, col_pass(u))
-    lax.fori_loop(0, NY, full, 0)
     settle(rsem, "p2", p2, NR - 1)
     v = mass_b / jnp.sum(p2[...], axis=0)
 
@@ -250,22 +267,26 @@
     settle(rsem, "y3", y3, 3)
     u = mass_a / jnp.sum(y3[...], axis=0)
     share("p3", p3, m, r_peers, col_pass(u))
+    forward("tgb", "fwb", RING8[3:])
     settle(rsem, "p3", p3, NR - 1)
     v = mass_b / jnp.sum(p3[...], axis=0)
 
     share("y4", y4, yc, y4_peers, row_pass(v))
+    settle(rsem, "fwb", tgt_all.at[0], 4)
+    lax.fori_loop(0, NY, full, 0)
     settle(rsem, "y4", y4, 3)
     sums = jnp.sum(y4[...], axis=0)
     u = mass_a / sums
-    share("p4", p4, m, r_peers, col_pass(u, keep=True))
-    weighted = nt(ste[...], wb[h])
-    den[m] = weighted[D : D + 1]
+    nothing = jnp.zeros((8, 128), F32)
+    sums_own = col_half(h, u, 0, nothing, keep=True)
+    weighted = nt(ste[...], wb[...])
     for n in range(NR):
         numt[n] = weighted[n * FR : n * FR + FR]
     num[m] = numt[m]
     for peer, index in zip(r_peers, r_index):
-        send("den", den.at[m], den.at[m], peer)
         send("num", numt.at[index], num.at[m], peer)
+    share("p4", p4, m, r_peers, both_halves(sums_own, col_half(1 - h, u, 0, nothing)))
+    share("den", den, m, r_peers, weighted[D : D + 1])
 
     f_last = f_own + log_a - jnp.log2(jnp.sum(y4[:, zi], axis=0)) + SHIFT
 
@@ -278,9 +299,8 @@
     g4 = g1 + jnp.log2(mass_b / jnp.sum(p4[...], axis=0))
     share("yg", yg, yc, y4_peers, g4)
 
-    settle(rsem, "den", den, NR - 1)
     settle(rsem, "num", num, NR - 1)
-    share("map", mapped, m, r_peers, jnp.sum(num[...], axis=0) / jnp.sum(den[...], axis=0))
+    share("map", mapped, m, r_peers, jnp.sum(num[...], axis=0))
 
     settle(rsem, "yg", yg, 3)
 
@@ -300,17 +320,30 @@
     both = lax.fori_loop(0, 4, finish, jnp.zeros((2 * D, S), F32))
     out_s[...] = both[:D] / both[D:]
 
+    settle(rsem, "den", den, NR - 1)
+    total = jnp.sum(den[...], axis=0)
     settle(rsem, "map", mapped, NR - 1)
     for n in range(NR):
-        out_t[n * FR : n * FR + FR, :] = mapped[n]
+        out_t[n * FR : n * FR + FR, :] = mapped[n] / total
 
     for name, buf, n in (
         ("y1", y1, 7), ("y2", y2, 7), ("y3", y3, 3), ("y4", y4, 3), ("yg", yg, 3), ("p1", p1, 7), ("z1", z1, 7),
         ("p2", p2, NR - 1), ("p3", p3, NR - 1), ("p4", p4, NR - 1), ("den", den, NR - 1), ("num", num, NR - 1),
         ("map", mapped, NR - 1), ("src", src_all, 3), ("fa", fa, 3), ("ga", ga, 1),
-        ("tgt", tgt_all.at[0], 7), ("fwd", tgt_all.at[0], 7),
+        ("tgt", tgt_all.at[0], 3), ("fwd", tgt_all.at[0], 3), ("tgb", tgt_all.at[0], 4), ("fwb", tgt_all.at[0], 4),
     ):
         settle(ssem, name, buf, n)
+
+
+def deliver(s_in, t_in, s_out, t_out, sems):
+    copies = [
+        pltpu.make_async_copy(s_in, s_out, sems.at[0]),
+        pltpu.make_async_copy(t_in, t_out, sems.at[1]),
+    ]
+    for copy in copies:
+        copy.start()
+    for copy in copies:
+        copy.wait()
 
 
 def per_device(source, target, log_source, log_target):
@@ -338,21 +371,34 @@
         pltpu.VMEM((T, S), F32),
         pltpu.VMEM((YH, ZH, T, S), F32),
         pltpu.VMEM((NY, T, S), F32),
-        pltpu.VMEM((YH, T, ZH * S), BF16),
+        pltpu.VMEM((T, ZH * S), BF16),
         pltpu.VMEM((2 * D, ZH * S), BF16),
+        pltpu.VMEM((D, S), BF16),
+        pltpu.VMEM((D, T), BF16),
+        pltpu.VMEM((1, S), F32),
+        pltpu.VMEM((1, T), F32),
         pltpu.SemaphoreType.DMA((n,)),
         pltpu.SemaphoreType.DMA((n,)),
+        pltpu.SemaphoreType.DMA((4,)),
     ]
     source_map, target_map = pl.pallas_call(
         kernel,
-        out_shape=(jax.ShapeDtypeStruct((D, S), F32), jax.ShapeDtypeStruct((D, T), F32)),
-        in_specs=[vmem] * 4,
+        out_shape=(pltpu.VMEM((D, S), F32), pltpu.VMEM((D, T), F32)),
+        in_specs=[pl.BlockSpec(memory_space=pltpu.HBM)] * 4,
         out_specs=(vmem, vmem),
         scratch_shapes=scratch,
         compiler_params=pltpu.CompilerParams(
-            collective_id=0, has_side_effects=True, vmem_limit_bytes=48 * 1024 * 1024
+            collective_id=0, has_side_effects=True, vmem_limit_bytes=62 * 1024 * 1024
         ),
     )(source.T, target.T, log_source.reshape(1, S), log_target.reshape(1, T))
+    source_map, target_map = pl.pallas_call(
+        deliver,
+        out_shape=(jax.ShapeDtypeStruct((D, S), F32), jax.ShapeDtypeStruct((D, T), F32)),
+        in_specs=[pl.BlockSpec(memory_space=pltpu.VMEM)] * 2,
+        out_specs=(pl.BlockSpec(memory_space=pl.ANY),) * 2,
+        scratch_shapes=[pltpu.SemaphoreType.DMA((2,))],
+        compiler_params=pltpu.CompilerParams(vmem_limit_bytes=2 * 1024 * 1024),
+    )(source_map, target_map)
     return source_map.T, target_map.T
 
 

time: 67 us -> 61.7 us (0.921)
  local copies, waits for them, and re-layouts: 3.56 us -> 0 us
  Pallas kernels: 62.5 us -> 60.9 us
    unnamed x10 -> x0, local copies, waits for them, and re-layouts: 3.56 us -> none
    pallas_call x1 -> x2, Pallas kernels: 62.5 us -> 60.9 us  [the longest x1 60.2 us: per_device(): pl.pallas_call(kernel, out_shape=(pltpu.VMEM((D, S), F32), pltpu.VMEM((D,...]
where the time goes in v3:
time: 61.7 us; the launch traced here: 61.5 us
  Pallas kernels  60.9 us (99%)
  between operations  0.64 us (1%)
    pallas_call x1, Pallas kernels, per_device(): pl.pallas_call(kernel, out_shape=(pltpu.VMEM((D, S), F32), pltpu.VMEM((D,...  60.2 us

profile of v3, /device:TPU:1, one launch (start us, length us, event | category | flops | bytes accessed | tf_op | source)
XLA Modules:
  0.0 61.5 jit_solution(11340633573282319444)
XLA Ops:
  0.6 60.2 %shard_map.59 = (f32[64,256]{1,0:T(8,128)S(1)}, f32[64,512]{1,0:T(8,128)S(1)}) custom-call(bf16[64,256]{1,0:T(8,128)(2,1)} %bitcast.7, bf16[64,512]{1,0:T(8,128)(2,1)} %bitcast.6, f32[1,256]{1,0:T(1,128)} %bitcast.9, f32[1,512]{1,0:T(1,128)} %bitcast.8), custom_call_target="tpu_custom_call" | custom-call | tf_op jit(solution)/shard_map/pallas_call | solution.py:384
  60.8 0.7 %shard_map.60 = (f32[64,256]{1,0:T(8,128)}, f32[64,512]{1,0:T(8,128)}) custom-call(f32[64,256]{1,0:T(8,128)S(1)} %get-tuple-element.6.s_in, f32[64,512]{1,0:T(8,128)S(1)} %get-tuple-element.7.t_in), custom_call_target="tpu_custom_call" | custom-call | tf_op jit(solution)/shard_map/pallas_call | solution.py:394

commit v4 on v3

--- a/solution.py
+++ b/solution.py
@@ -23,7 +23,7 @@
 PLANE = tuple((dx, dc) for dx in (2, 1, 3) for dc in (1, 0)) + ((0, 1),)
 
 PHASES = (
-    "y1", "y2", "y3", "y4", "yg", "p1", "z1", "p2", "p3", "p4", "den", "num", "map", "src", "fa", "ga", "tgt", "fwd",
+    "y1", "y2", "y3", "y4", "p1", "z1", "p2", "p3", "p4", "den", "num", "map", "src", "fa", "ga", "tgt", "fwd",
     "tgb", "fwb",
 )
 IDX = {name: i for i, name in enumerate(PHASES)}
@@ -73,7 +73,7 @@
 def kernel(
     src_hbm, tgt_hbm, ls_hbm, lt_hbm, out_s, out_t,
     y1, y2, y3, y4, yg, p1, z1, p2, p3, p4, den, num, mapped, src_all, fa, ga, tgt_all,
-    numt, mt_own, k_ref, mf, wb, ste, src_ref, tgt_ref, ls_ref, lt_ref, ssem, rsem, isem,
+    numt, mt_own, k_ref, mf, wb, ste, src_ref, tgt_ref, ls_ref, lt_ref, both, ssem, rsem, isem, gsem,
 ):
     row, y = lax.axis_index("row"), lax.axis_index("col")
     x, z, c = row // (NZ * NC), lax.rem(row // NC, NZ), lax.rem(row, NC)
@@ -175,9 +175,6 @@
     settle(rsem, "src", src_all, 3)
     settle(rsem, "fa", fa, 3)
     mass_a = jnp.exp2(fa[:, :, S:])
-    ste[D:, :] = jnp.ones((D, ZH * S), BF16)
-    for zz in range(ZH):
-        ste[:D, zz * S : (zz + 1) * S] = src_all[zz].astype(BF16)
 
     def fill(half, points):
         for zz in range(ZH):
@@ -192,8 +189,6 @@
         for d in distances:
             other = lax.rem(y + d, NY)
             send(name, tgt_all.at[c, other], tgt_all.at[c, other], sibling)
-
-    forward("tgt", "fwd", RING8[:3])
 
     def build(half, potential, acc):
         for k in range(NK):
@@ -211,16 +206,10 @@
                 acc = acc + k_ref[half, :, 8 * k : 8 * k + 8, :] * v[:, n : n + 1]
         return jnp.sum(acc, axis=1, keepdims=True)
 
-    def col_half(half, u, first, out, keep=False):
+    def col_half(half, u, first, out):
         ub = jnp.broadcast_to(u, (ZH, 8, S))
         for k in range(NK):
             block = k_ref[half, :, 8 * k : 8 * k + 8, :] * ub
-            if keep and k % 2 == 0:
-                before = block
-            elif keep:
-                for zz in range(ZH):
-                    pair = jnp.concatenate([before[zz], block[zz]], axis=0)
-                    wb[8 * k - 8 : 8 * k + 8, zz * S : (zz + 1) * S] = pair.astype(BF16)
             t = jnp.sum(block, axis=0)
             t = t[:, :128] + t[:, 128:]
             out = jnp.where(lane == first + k, jnp.sum(t, axis=1, keepdims=True), out)
@@ -231,10 +220,11 @@
 
     settle(rsem, "z1", z1, 7)
     g1_own = log_b_own - lse2(z1[...])
+    ga[0] = jnp.concatenate([g1_own, log_b_own], axis=0)
+    send("ga", ga.at[0], ga.at[1], place(x, z, c, lax.rem(y + 4, NY)))
     acc = build(h, g1_own, jnp.zeros((ZH, 8, S), F32))
     share("y2", y2, y, y_peers, jnp.sum(acc, axis=1, keepdims=True))
-    ga[0] = jnp.concatenate([g1_own, log_b_own], axis=0)
-    send("ga", ga.at[0], ga.at[1], place(x, z, c, lax.rem(y + 4, NY)))
+    forward("tgt", "fwd", RING8[:3])
     settle(rsem, "fwd", tgt_all.at[0], 3)
 
     def full(yy, carry):
@@ -274,18 +264,25 @@
     share("y4", y4, yc, y4_peers, row_pass(v))
     settle(rsem, "fwb", tgt_all.at[0], 4)
     lax.fori_loop(0, NY, full, 0)
+    for zz in range(ZH):
+        wb[:, zz * S : (zz + 1) * S] = k_ref[h, zz].astype(BF16)
     settle(rsem, "y4", y4, 3)
     sums = jnp.sum(y4[...], axis=0)
     u = mass_a / sums
-    nothing = jnp.zeros((8, 128), F32)
-    sums_own = col_half(h, u, 0, nothing, keep=True)
+    for zz in range(ZH):
+        mass = jnp.broadcast_to(u[zz], (16, S))
+        scaled = jnp.concatenate([src_all[zz] * u[zz], mass], axis=0)
+        high = scaled.astype(BF16)
+        low = (scaled - high.astype(F32)).astype(BF16)
+        ste[:, zz * S : (zz + 1) * S] = jnp.concatenate([high, low], axis=0)
     weighted = nt(ste[...], wb[...])
+    weighted = weighted[: D + 16] + weighted[D + 16 :]
     for n in range(NR):
         numt[n] = weighted[n * FR : n * FR + FR]
     num[m] = numt[m]
     for peer, index in zip(r_peers, r_index):
         send("num", numt.at[index], num.at[m], peer)
-    share("p4", p4, m, r_peers, both_halves(sums_own, col_half(1 - h, u, 0, nothing)))
+    share("p4", p4, m, r_peers, col_pass(u))
     share("den", den, m, r_peers, weighted[D : D + 1])
 
     f_last = f_own + log_a - jnp.log2(jnp.sum(y4[:, zi], axis=0)) + SHIFT
@@ -297,15 +294,19 @@
     lax.fori_loop(0, NY, add_f, 0)
     settle(rsem, "p4", p4, NR - 1)
     g4 = g1 + jnp.log2(mass_b / jnp.sum(p4[...], axis=0))
-    share("yg", yg, yc, y4_peers, g4)
+    yg[yc] = g4
+    for i, peer in enumerate(y4_peers):
+        pltpu.make_async_remote_copy(
+            src_ref=yg.at[yc], dst_ref=yg.at[yc], send_sem=gsem.at[i], recv_sem=gsem.at[3 + i],
+            device_id=peer, device_id_type=MESH,
+        ).start()
 
     settle(rsem, "num", num, NR - 1)
     share("map", mapped, m, r_peers, jnp.sum(num[...], axis=0))
 
-    settle(rsem, "yg", yg, 3)
-
-    def finish(cls, acc):
+    def finish(cls):
         potential = yg[cls]
+        acc = jnp.zeros((2 * D, S), F32)
         for half in range(YH):
             yy = cls + 4 * half
             parts = []
@@ -315,10 +316,15 @@
             weight = jnp.concatenate(parts, axis=0).astype(BF16)
             block = jnp.concatenate([tgt_all[0, yy], tgt_all[1, yy], jnp.ones((D, T), F32)], axis=0)
             acc = acc + nn(block.astype(BF16), weight)
-        return acc
-
-    both = lax.fori_loop(0, 4, finish, jnp.zeros((2 * D, S), F32))
-    out_s[...] = both[:D] / both[D:]
+        both[cls] = acc
+
+    finish(yc)
+    for i, d in ((2, 1), (1, 7), (0, 6)):
+        cls = lax.rem(y + d, 4)
+        pltpu.make_async_copy(yg.at[cls], yg.at[cls], gsem.at[3 + i]).wait()
+        finish(cls)
+    maps = jnp.sum(both[...], axis=0)
+    out_s[...] = maps[:D] / maps[D:]
 
     settle(rsem, "den", den, NR - 1)
     total = jnp.sum(den[...], axis=0)
@@ -327,12 +333,14 @@
         out_t[n * FR : n * FR + FR, :] = mapped[n] / total
 
     for name, buf, n in (
-        ("y1", y1, 7), ("y2", y2, 7), ("y3", y3, 3), ("y4", y4, 3), ("yg", yg, 3), ("p1", p1, 7), ("z1", z1, 7),
+        ("y1", y1, 7), ("y2", y2, 7), ("y3", y3, 3), ("y4", y4, 3), ("p1", p1, 7), ("z1", z1, 7),
         ("p2", p2, NR - 1), ("p3", p3, NR - 1), ("p4", p4, NR - 1), ("den", den, NR - 1), ("num", num, NR - 1),
         ("map", mapped, NR - 1), ("src", src_all, 3), ("fa", fa, 3), ("ga", ga, 1),
         ("tgt", tgt_all.at[0], 3), ("fwd", tgt_all.at[0], 3), ("tgb", tgt_all.at[0], 4), ("fwb", tgt_all.at[0], 4),
     ):
         settle(ssem, name, buf, n)
+    for i in range(3):
+        pltpu.make_async_copy(yg.at[0], yg.at[0], gsem.at[i]).wait()
 
 
 def deliver(s_in, t_in, s_out, t_out, sems):
@@ -372,14 +380,16 @@
         pltpu.VMEM((YH, ZH, T, S), F32),
         pltpu.VMEM((NY, T, S), F32),
         pltpu.VMEM((T, ZH * S), BF16),
-        pltpu.VMEM((2 * D, ZH * S), BF16),
+        pltpu.VMEM((2 * (D + 16), ZH * S), BF16),
         pltpu.VMEM((D, S), BF16),
         pltpu.VMEM((D, T), BF16),
         pltpu.VMEM((1, S), F32),
         pltpu.VMEM((1, T), F32),
+        pltpu.VMEM((4, 2 * D, S), F32),
         pltpu.SemaphoreType.DMA((n,)),
         pltpu.SemaphoreType.DMA((n,)),
         pltpu.SemaphoreType.DMA((4,)),
+        pltpu.SemaphoreType.DMA((6,)),
     ]
     source_map, target_map = pl.pallas_call(
         kernel,

time: 61.7 us -> 60.3 us (0.977)
  Pallas kernels: 60.9 us -> 59.5 us
    pallas_call x1, Pallas kernels: 60.2 us -> 58.8 us  [per_device(): pl.pallas_call(kernel, out_shape=(pltpu.VMEM((D, S), F32), pltpu.VMEM((D,...]
where the time goes in v4:
time: 60.3 us; the launch traced here: 60.1 us
  Pallas kernels  59.5 us (99%)
  between operations  0.64 us (1%)
    pallas_call x1, Pallas kernels, per_device(): pl.pallas_call(kernel, out_shape=(pltpu.VMEM((D, S), F32), pltpu.VMEM((D,...  58.8 us

profile of v4, /device:TPU:1, one launch (start us, length us, event | category | flops | bytes accessed | tf_op | source)
XLA Modules:
  0.0 60.1 jit_solution(11053917784931237868)
XLA Ops:
  0.6 58.8 %shard_map.59 = (f32[64,256]{1,0:T(8,128)S(1)}, f32[64,512]{1,0:T(8,128)S(1)}) custom-call(bf16[64,256]{1,0:T(8,128)(2,1)} %bitcast.7, bf16[64,512]{1,0:T(8,128)(2,1)} %bitcast.6, f32[1,256]{1,0:T(1,128)} %bitcast.9, f32[1,512]{1,0:T(1,128)} %bitcast.8), custom_call_target="tpu_custom_call" | custom-call | tf_op jit(solution)/shard_map/pallas_call | solution.py:394
  59.4 0.7 %shard_map.60 = (f32[64,256]{1,0:T(8,128)}, f32[64,512]{1,0:T(8,128)}) custom-call(f32[64,256]{1,0:T(8,128)S(1)} %get-tuple-element.6.s_in, f32[64,512]{1,0:T(8,128)S(1)} %get-tuple-element.7.t_in), custom_call_target="tpu_custom_call" | custom-call | tf_op jit(solution)/shard_map/pallas_call | solution.py:404

commit v5 on v4

--- a/solution.py
+++ b/solution.py
@@ -109,12 +109,13 @@
             ((src_hbm, src_ref), (tgt_hbm, tgt_ref), (ls_hbm, ls_ref), (lt_hbm, lt_ref))
         )
     ]
-    for load in loads:
-        load.start()
     barrier = pltpu.get_barrier_semaphore()
     greeted = y_peers + z_peers + g_peers + [place(px, z_pair, pc, y) for px, pc in far_pos[:-1]]
     for peer in greeted:
         pl.semaphore_signal(barrier, inc=1, device_id=peer, device_id_type=MESH)
+
+    for load in loads:
+        load.start()
 
     def send(name, source, target, peer):
         i = IDX[name]
@@ -292,6 +293,8 @@
         return carry
 
     lax.fori_loop(0, NY, add_f, 0)
+    settle(rsem, "num", num, NR - 1)
+    share("map", mapped, m, r_peers, jnp.sum(num[...], axis=0))
     settle(rsem, "p4", p4, NR - 1)
     g4 = g1 + jnp.log2(mass_b / jnp.sum(p4[...], axis=0))
     yg[yc] = g4
@@ -300,9 +303,6 @@
             src_ref=yg.at[yc], dst_ref=yg.at[yc], send_sem=gsem.at[i], recv_sem=gsem.at[3 + i],
             device_id=peer, device_id_type=MESH,
         ).start()
-
-    settle(rsem, "num", num, NR - 1)
-    share("map", mapped, m, r_peers, jnp.sum(num[...], axis=0))
 
     def finish(cls):
         potential = yg[cls]

time: 60.3 us -> 59.7 us (0.990)
  no operation moved by 1% of the time
where the time goes in v5:
time: 59.7 us; the launch traced here: 59.6 us
  Pallas kernels  58.9 us (99%)
  between operations  0.64 us (1%)
    pallas_call x1, Pallas kernels, per_device(): pl.pallas_call(kernel, out_shape=(pltpu.VMEM((D, S), F32), pltpu.VMEM((D,...  58.2 us

profile of v5, /device:TPU:1, one launch (start us, length us, event | category | flops | bytes accessed | tf_op | source)
XLA Modules:
  0.0 59.6 jit_solution(5296713171616814800)
XLA Ops:
  0.6 58.2 %shard_map.59 = (f32[64,256]{1,0:T(8,128)S(1)}, f32[64,512]{1,0:T(8,128)S(1)}) custom-call(bf16[64,256]{1,0:T(8,128)(2,1)} %bitcast.7, bf16[64,512]{1,0:T(8,128)(2,1)} %bitcast.6, f32[1,256]{1,0:T(1,128)} %bitcast.9, f32[1,512]{1,0:T(1,128)} %bitcast.8), custom_call_target="tpu_custom_call" | custom-call | tf_op jit(solution)/shard_map/pallas_call | solution.py:394
  58.9 0.7 %shard_map.60 = (f32[64,256]{1,0:T(8,128)}, f32[64,512]{1,0:T(8,128)}) custom-call(f32[64,256]{1,0:T(8,128)S(1)} %get-tuple-element.6.s_in, f32[64,512]{1,0:T(8,128)S(1)} %get-tuple-element.7.t_in), custom_call_target="tpu_custom_call" | custom-call | tf_op jit(solution)/shard_map/pallas_call | solution.py:404

commit v6 on v5

--- a/solution.py
+++ b/solution.py
@@ -270,6 +270,7 @@
     settle(rsem, "y4", y4, 3)
     sums = jnp.sum(y4[...], axis=0)
     u = mass_a / sums
+    share("p4", p4, m, r_peers, col_pass(u))
     for zz in range(ZH):
         mass = jnp.broadcast_to(u[zz], (16, S))
         scaled = jnp.concatenate([src_all[zz] * u[zz], mass], axis=0)
@@ -283,7 +284,6 @@
     num[m] = numt[m]
     for peer, index in zip(r_peers, r_index):
         send("num", numt.at[index], num.at[m], peer)
-    share("p4", p4, m, r_peers, col_pass(u))
     share("den", den, m, r_peers, weighted[D : D + 1])
 
     f_last = f_own + log_a - jnp.log2(jnp.sum(y4[:, zi], axis=0)) + SHIFT

time: 59.7 us -> 60.1 us (level)
  no operation moved by 1% of the time
where the time goes in v6:
time: 60.1 us; the launch traced here: 59.9 us
  Pallas kernels  59.3 us (99%)
  between operations  0.64 us (1%)
    pallas_call x1, Pallas kernels, per_device(): pl.pallas_call(kernel, out_shape=(pltpu.VMEM((D, S), F32), pltpu.VMEM((D,...  58.6 us

profile of v6, /device:TPU:1, one launch (start us, length us, event | category | flops | bytes accessed | tf_op | source)
XLA Modules:
  0.0 59.9 jit_solution(3708855964057311344)
XLA Ops:
  0.6 58.6 %shard_map.59 = (f32[64,256]{1,0:T(8,128)S(1)}, f32[64,512]{1,0:T(8,128)S(1)}) custom-call(bf16[64,256]{1,0:T(8,128)(2,1)} %bitcast.7, bf16[64,512]{1,0:T(8,128)(2,1)} %bitcast.6, f32[1,256]{1,0:T(1,128)} %bitcast.9, f32[1,512]{1,0:T(1,128)} %bitcast.8), custom_call_target="tpu_custom_call" | custom-call | tf_op jit(solution)/shard_map/pallas_call | solution.py:394
  59.2 0.7 %shard_map.60 = (f32[64,256]{1,0:T(8,128)}, f32[64,512]{1,0:T(8,128)}) custom-call(f32[64,256]{1,0:T(8,128)S(1)} %get-tuple-element.6.s_in, f32[64,512]{1,0:T(8,128)S(1)} %get-tuple-element.7.t_in), custom_call_target="tpu_custom_call" | custom-call | tf_op jit(solution)/shard_map/pallas_call | solution.py:404
